TPU v7x, 128 devices: a whole 4x4x4 slice. The times are simulated.
128 devices in a mesh: row: 8 (over z, core), col: 16 (over y, x).
Axes of the slice: x: 4, y: 4, z: 4, core: 2. Of those that a mesh axis runs over, the one named last changes fastest.
Arguments:
- vectors: bfloat16 [32, 32, 16, 256], P('row', 'col'), may hold values from -6 to 6
- near_blocks: bfloat16 [32, 32, 9, 256, 256], P('row', 'col'), may hold values from -0.125 to 0.125
- near_mask: int32 [32, 32, 8], P('row', 'col'), may hold values 0 or 1
- far_mask: int32 [32, 32, 16], P('row', 'col'), may hold values 0 or 1
- leaf_basis: bfloat16 [32, 32, 256, 64], P('row', 'col'), may hold values from -0.375 to 0.375
- far_transfer: bfloat16 [24, 64, 64], replicated, may hold values from -0.15625 to 0.15625
- coarse_basis: bfloat16 [32, 32, 64, 256], P('row', 'col'), may hold values from -0.25 to 0.25
- coarse_list: int32 [128, 8], P(('row', 'col')), may hold values from 0 to 127, as said below
- coarse_transfer: float32 [128, 8, 256, 256], P(('row', 'col')), may hold values from -0.125 to 0.125
Outputs:
- applied: float32 [32, 32, 16, 256], P('row', 'col')
Inputs may be any that keep to these rules, and one draw needn't show every extreme that they name: `coarse_list`: each row lists 8 distinct coarse clusters, never its own; cluster d is the device with row index d // 16 and col index d % 16. Every listed cluster's row index and col index each differ from those of d by at most 2.
All inputs are finite; a program needn't handle non-finite values. No bound on the sum of `near_mask` or of `far_mask` on one device may be relied on, other than what follows from the above.
Results may differ from a plain program's by a relative error of at most 0.003.
Values may be sent and summed in bfloat16 or wider, within the bound.
A program may use at most 64 MiB of HBM per device.

v0:
```python
import jax
import jax.numpy as jnp
from jax import lax
from jax.sharding import PartitionSpec as P

NEAR_OFFSETS = [(step_a, step_b) for step_a in (-1, 0, 1) for step_b in (-1, 0, 1)]
FAR_OFFSETS = [
    (step_a, step_b)
    for step_a in (-2, -1, 0, 1, 2)
    for step_b in (-2, -1, 0, 1, 2)
    if (step_a, step_b) != (0, 0)
]


def extended(cells, sides, width):
    for axis, dim in sides:
        count = lax.axis_size(axis)
        ends = count - 1
        head = lax.slice_in_dim(cells, 0, width, axis=dim)
        tail = lax.slice_in_dim(cells, cells.shape[dim] - width, cells.shape[dim], axis=dim)
        cells = jnp.concatenate(
            [
                lax.ppermute(tail, axis, [(i, (i + 1) % count) for i in range(ends)]),
                cells,
                lax.ppermute(head, axis, [((i + 1) % count, i) for i in range(ends)]),
            ],
            axis=dim,
        )
    return cells


def near_live(near_mask):
    ones_col = jnp.ones(near_mask.shape[:2] + (1,), jnp.int32)
    return jnp.concatenate([near_mask[:, :, :4], ones_col, near_mask[:, :, 4:]], axis=2)


def far_weights(near_mask, far_mask):
    columns = []
    cycle_one = 0
    cycle_two = 0
    for step_a, step_b in FAR_OFFSETS:
        if max(abs(step_a), abs(step_b)) == 1:
            columns.append(1 - near_mask[:, :, cycle_one])
            cycle_one += 1
        else:
            columns.append(far_mask[:, :, cycle_two])
            cycle_two += 1
    return jnp.stack(columns, axis=2)


def per_device(
    vectors,
    near_blocks,
    near_mask,
    far_mask,
    leaf_basis,
    far_transfer,
    coarse_basis,
    coarse_list,
    coarse_transfer,
):
    size_x = vectors.shape[0]
    size_y = vectors.shape[1]
    vec_wide = extended(vectors, (("row", 0), ("col", 1)), 1)
    coeffs = jnp.einsum(
        "xyrl,xylk->xyrk", vectors, leaf_basis, preferred_element_type=jnp.float32
    ).astype(jnp.bfloat16)
    coeff_wide = extended(coeffs, (("row", 0), ("col", 1)), 2)
    live = near_live(near_mask).astype(jnp.bfloat16)
    stacked_near = jnp.stack(
        [
            vec_wide[1 + step_a : 1 + step_a + size_x, 1 + step_b : 1 + step_b + size_y]
            for step_a, step_b in NEAR_OFFSETS
        ],
        axis=2,
    )
    stacked_near = stacked_near * live[:, :, :, None, None]
    near = jnp.einsum(
        "xysrl,xyslm->xyrm", stacked_near, near_blocks, preferred_element_type=jnp.float32
    )
    weight = far_weights(near_mask, far_mask).astype(jnp.bfloat16)
    stacked_far = jnp.stack(
        [
            coeff_wide[2 + step_a : 2 + step_a + size_x, 2 + step_b : 2 + step_b + size_y]
            for step_a, step_b in FAR_OFFSETS
        ],
        axis=2,
    )
    stacked_far = stacked_far * weight[:, :, :, None, None]
    local_leaf = jnp.einsum(
        "xyors,osk->xyrk", stacked_far, far_transfer, preferred_element_type=jnp.float32
    )
    coarse_own = jnp.einsum(
        "xyrk,xykj->rj", coeffs, coarse_basis, preferred_element_type=jnp.float32
    )
    own_list = coarse_list[0]
    own_transfer = coarse_transfer[0]
    total_dev = lax.axis_size("row") * lax.axis_size("col")
    all_coarse = lax.all_gather(coarse_own[None], ("row", "col"), axis=0, tiled=True)
    selector = (own_list[:, None] == jnp.arange(total_dev, dtype=jnp.int32)[None, :]).astype(
        jnp.float32
    )
    picked = jnp.einsum("fd,drj->frj", selector, all_coarse, precision=lax.Precision.HIGHEST)
    coarse_local = jnp.einsum("frs,fsk->rk", picked, own_transfer, precision=lax.Precision.HIGHEST)
    coarse_local = coarse_local.astype(jnp.bfloat16)
    downward = jnp.einsum(
        "rj,xykj->xyrk", coarse_local, coarse_basis, preferred_element_type=jnp.float32
    )
    local_all = (local_leaf + downward).astype(jnp.bfloat16)
    far_part = jnp.einsum(
        "xyrk,xylk->xyrl", local_all, leaf_basis, preferred_element_type=jnp.float32
    )
    return near + far_part


def solution(mesh):
    placed = (
        P("row", "col", None, None),
        P("row", "col", None, None, None),
        P("row", "col", None),
        P("row", "col", None),
        P("row", "col", None, None),
        P(),
        P("row", "col", None, None),
        P(("row", "col"), None),
        P(("row", "col"), None, None, None),
    )
    return jax.shard_map(
        per_device,
        mesh=mesh,
        in_specs=placed,
        out_specs=P("row", "col", None, None),
        check_vma=False,
    )
```

profile of v0, /device:TPU:1, one launch (start us, length us, event | category | flops | bytes accessed | tf_op | source)
XLA Modules:
  0.0 91.6 jit_solution(1288099628486143720)
XLA Ops:
  6.5 1.3 %convolution_convert_fusion = bf16[4,2,16,64]{3,2,1,0:T(8,128)(2,1)S(1)} fusion(bf16[4,2,16,256]{3,2,1,0:T(8,128)(2,1)} %param.9, bf16[4,2,256,64]{2,3,1,0:T(8,128)(2,1)} %param.13), kind=kOutput, calls=%fused_computation.10 | convolution fusion | flops 4202496 | bytes 344064 | tf_op jit(solution)/shard_map/xyrl,xylk->xyrk/dot_general | solution.py:65
  7.8 1.8 %convolution_bitcast_fusion.1 = f32[16,256]{1,0:T(8,128)} fusion(bf16[4,2,16,64]{3,2,1,0:T(8,128)(2,1)S(1)} %convolution_convert_fusion, bf16[4,2,64,256]{3,2,1,0:T(8,128)(2,1)} %param.15), kind=kOutput, calls=%fused_computation.12 | convolution fusion | flops 4194304 | bytes 294912 | tf_op jit(solution)/shard_map/xyrk,xykj->rj/dot_general | solution.py:93
  9.6 0.0 all-gather.3.cloned.1.call-update
  9.6 0.7 fusion.46
  10.4 4.9 %collective-permute-start = (bf16[1,2,16,256]{3,2,1,0:T(8,128)(2,1)S(1)}, bf16[1,2,16,256]{3,2,1,0:T(8,128)(2,1)S(1)}, u32[]{:S(2)}, u32[]{:S(2)}) collective-permute-start(bf16[1,2,16,256]{3,2,1,0:T(8,128)(2,1)S(1)} %get-tuple-element.10), channel_id=1, source_target_pairs={{0,16},{16,32},{32,48},{48,64},{64,80},{80,96},{96,112},{1,17},{17... | collective-permute-start | bytes 49160 | tf_op jit(solution)/shard_map/ppermute | solution.py:23
  15.3 1.9 %collective-permute-start.1 = (bf16[1,2,16,256]{3,2,1,0:T(8,128)(2,1)S(1)}, bf16[1,2,16,256]{3,2,1,0:T(8,128)(2,1)S(1)}, u32[]{:S(2)}, u32[]{:S(2)}) collective-permute-start(bf16[1,2,16,256]{3,2,1,0:T(8,128)(2,1)S(1)} %get-tuple-element.9), channel_id=1, source_target_pairs={{16,0},{32,16},{48,32},{64,48},{80,64},{96,80},{112,96},{17,1},{33... | collective-permute-start | bytes 49160 | tf_op jit(solution)/shard_map/ppermute | solution.py:25
  17.2 1.9 %collective-permute-start.5 = (bf16[2,2,16,64]{3,2,1,0:T(8,128)(2,1)S(1)}, bf16[2,2,16,64]{3,2,1,0:T(8,128)(2,1)S(1)}, u32[]{:S(2)}, u32[]{:S(2)}) collective-permute-start(bf16[2,2,16,64]{3,2,1,0:T(8,128)(2,1)S(1)} %get-tuple-element.12), channel_id=1, source_target_pairs={{16,0},{32,16},{48,32},{64,48},{80,64},{96,80},{112,96},{17,1},{33... | collective-permute-start | bytes 24584 | tf_op jit(solution)/shard_map/ppermute | solution.py:25
  19.2 3.6 %collective-permute-start.4 = (bf16[2,2,16,64]{3,2,1,0:T(8,128)(2,1)S(1)}, bf16[2,2,16,64]{3,2,1,0:T(8,128)(2,1)S(1)}, u32[]{:S(2)}, u32[]{:S(2)}) collective-permute-start(bf16[2,2,16,64]{3,2,1,0:T(8,128)(2,1)S(1)} %get-tuple-element.11), channel_id=1, source_target_pairs={{0,16},{16,32},{32,48},{48,64},{64,80},{80,96},{96,112},{1,17},{17... | collective-permute-start | bytes 24584 | tf_op jit(solution)/shard_map/ppermute | solution.py:23
  22.8 0.7 convert.42
  23.5 1.1 %fusion.48 = (s32[4,2,1]{2,1,0:T(2,128)S(1)}, s32[4,2,1]{2,1,0:T(2,128)S(1)}, s32[4,2,1]{2,1,0:T(2,128)S(1)}, s32[4,2,1]{2,1,0:T(2,128)S(1)}, s32[4,2,1]{2,1,0:T...) fusion(s32[4,2,8]{2,1,0:T(2,128)} %param.11), kind=kLoop, calls=%fused_computation.134 | loop fusion | bytes 512 | tf_op jit(solution)/shard_map/slice | solution.py:43
  24.6 0.7 convert.43
  25.3 0.1 fusion.49
  25.4 0.1 fusion.50
  25.4 0.1 fusion.51
  25.5 0.1 copy.43
  25.6 0.1 copy.44
  25.7 0.1 copy.45
  25.8 0.1 copy.46
  25.9 0.1 copy.47
  26.1 0.1 copy.48
  26.2 0.1 copy.49
  26.3 0.1 copy.50
  26.4 0.1 pad.16.clone
  26.4 0.1 pad_maximum_fusion.8
  26.5 0.1 copy.13
  26.7 0.1 copy.23
  26.8 0.1 copy.24
  26.9 0.1 copy.25
  27.0 0.1 copy.26
  27.1 0.1 copy.27
  27.2 0.1 copy.28
  27.3 0.1 copy.29
  27.4 0.1 copy.30
  27.6 0.1 stack.152
  27.7 0.1 copy.31
  27.9 3.1 %collective-permute-start.6 = (bf16[8,2,16,64]{3,2,1,0:T(8,128)(2,1)S(1)}, bf16[8,2,16,64]{3,2,1,0:T(8,128)(2,1)S(1)}, u32[]{:S(2)}, u32[]{:S(2)}) collective-permute-start(bf16[8,2,16,64]{3,2,1,0:T(8,128)(2,1)S(1)} %pad_maximum_fusion.5), channel_id=1, source_target_pairs={{0,1},{1,2},{2,3},{3,4},{4,5},{5,6},{6,7},{7,8},{8,9},{9,10},{10,1... | collective-permute-start | bytes 98312 | tf_op jit(solution)/shard_map/ppermute | solution.py:23
  31.0 1.3 %collective-permute-start.7 = (bf16[8,2,16,64]{3,2,1,0:T(8,128)(2,1)S(1)}, bf16[8,2,16,64]{3,2,1,0:T(8,128)(2,1)S(1)}, u32[]{:S(2)}, u32[]{:S(2)}) collective-permute-start(bf16[8,2,16,64]{3,2,1,0:T(8,128)(2,1)S(1)} %pad_maximum_fusion.5), channel_id=1, source_target_pairs={{1,0},{2,1},{3,2},{4,3},{5,4},{6,5},{7,6},{8,7},{9,8},{10,9},{11,1... | collective-permute-start | bytes 98312 | tf_op jit(solution)/shard_map/ppermute | solution.py:25
  32.3 0.8 constant_dynamic-update-slice_fusion.1
  33.2 4.0 %collective-permute-start.2 = (bf16[6,1,16,256]{3,2,1,0:T(8,128)(2,1)S(1)}, bf16[6,1,16,256]{3,2,1,0:T(8,128)(2,1)S(1)}, u32[]{:S(2)}, u32[]{:S(2)}) collective-permute-start(bf16[6,1,16,256]{3,2,1,0:T(8,128)(2,1)S(1)} %get-tuple-element.6), channel_id=1, source_target_pairs={{0,1},{1,2},{2,3},{3,4},{4,5},{5,6},{6,7},{7,8},{8,9},{9,10},{10,1... | collective-permute-start | bytes 147464 | tf_op jit(solution)/shard_map/ppermute | solution.py:23
  37.2 1.3 %collective-permute-start.3 = (bf16[6,1,16,256]{3,2,1,0:T(8,128)(2,1)S(1)}, bf16[6,1,16,256]{3,2,1,0:T(8,128)(2,1)S(1)}, u32[]{:S(2)}, u32[]{:S(2)}) collective-permute-start(bf16[6,1,16,256]{3,2,1,0:T(8,128)(2,1)S(1)} %get-tuple-element.5), channel_id=1, source_target_pairs={{1,0},{2,1},{3,2},{4,3},{5,4},{6,5},{7,6},{8,7},{9,8},{10,9},{11,1... | collective-permute-start | bytes 147464 | tf_op jit(solution)/shard_map/ppermute | solution.py:25
  38.7 0.0 copy-start.1
  39.0 0.5 fusion.17
  39.6 3.2 %collective-permute-done.3 = bf16[6,1,16,256]{3,2,1,0:T(8,128)(2,1)S(1)} collective-permute-done((bf16[6,1,16,256]{3,2,1,0:T(8,128)(2,1)S(1)}, bf16[6,1,16,256]{3,2,1,0:T(8,128)(2,1)S(1)}, u32[]{:S(2)}, u32[]{:S(2)}) %collective-permute-start.3) | collective-permute-done | bytes 49184 | tf_op jit(solution)/shard_map/ppermute | solution.py:25
  42.9 4.6 %fusion = f32[4,2,16,256,1]{3,2,0,1,4:T(8,128)S(1)} fusion(bf16[4,2,9,256,256]{4,3,2,1,0:T(8,128)(2,1)} %param.10, bf16[4,2,9,16,256]{4,3,1,0,2:T(8,128)(2,1)S(1)} %constant_dynamic-update-slice_fusion.3, bf16[4,2,9]{1,0,2:T(4,128)(2,1)S(1)} %copy.13), kind=kOutput, calls=%fused_computation | convolution fusion | flops 151289856 | bytes 10158224 | tf_op jit(solution)/shard_map/xysrl,xyslm->xyrm/dot_general | solution.py:78
  47.5 31.8 %all-gather.3.cloned.1.call-done = f32[2048,256]{1,0:T(8,128)} async-done(((f32[16,256]{1,0:T(8,128)}), f32[2048,256]{1,0:T(8,128)}) %all-gather.3.cloned.1.call-update) | async-done | bytes 2097168 | tf_op jit(solution)/shard_map/all_gather | solution.py:99
  79.3 3.5 %fusion.4 = f32[8,16,256]{2,0,1:T(8,128)S(1)} fusion(f32[128,16,256]{2,1,0:T(8,128)} %bitcast.186, s32[8]{0:T(128)S(1)} %bitcast.187), kind=kOutput, calls=%fused_computation.4 | convolution fusion | flops 50332672 | bytes 2228256 | tf_op jit(solution)/shard_map/fd,drj->frj/dot_general | solution.py:103
  82.8 0.9 %fusion.14 = bf16[16,256,1,1]{1,0,3,2:T(8,128)(2,1)S(1)} fusion(f32[1,8,256,256]{3,2,1,0:T(8,128)S(1)} %copy-done, f32[8,16,256]{2,0,1:T(8,128)S(1)} %fusion.4), kind=kOutput, calls=%fused_computation.14 | convolution fusion | flops 100667392 | bytes 2236416 | tf_op jit(solution)/shard_map/frs,fsk->rk/dot_general | solution.py:104
  83.8 1.0 %convolution_add_fusion = f32[4,2,16,256]{3,2,1,0:T(8,128)} fusion(bf16[4,2,256,64]{2,3,1,0:T(8,128)(2,1)S(1)} %copy-done.2, bf16[16,256,1,1]{1,0,3,2:T(8,128)(2,1)S(1)} %fusion.14, bf16[4,2,64,256]{3,2,1,0:T(8,128)(2,1)S(1)} %copy-done.3, f32[4,2,16,256,1]{3,2,0,1,4:T(8,128)S(1)} %fusion, f32[4,2,16,64,1]{3,2,0,1,4:T(8,128)S(1)} %fusion.17), kind=kOutput, calls=%fused_computation.6 | convolution fusion | flops 8437760 | bytes 827392 | tf_op jit(solution)/shard_map/xyrk,xylk->xyrl/dot_general | solution.py:110
  (66 shorter events, 0.5 us)
Async XLA Ops:
  6.5 76.3 %copy-start = (f32[1,8,256,256]{3,2,1,0:T(8,128)S(1)}, f32[1,8,256,256]{3,2,1,0:T(8,128)}, u32[]{:S(2)}) copy-start(f32[1,8,256,256]{3,2,1,0:T(8,128)} %param.17) | copy-start | bytes 6291460
  6.5 32.5 %copy-start.5 = (bf16[24,64,64]{2,1,0:T(8,128)(2,1)S(1)}, bf16[24,64,64]{2,1,0:T(8,128)(2,1)}, u32[]{:S(2)}) copy-start(bf16[24,64,64]{2,1,0:T(8,128)(2,1)} %param.14) | copy-start | bytes 589828
  6.5 72.8 %all-gather.3.cloned.1.call-start = ((), (), s32[]{:S(2)}) async-start(), calls=%async_computation | async-start | bytes 2113536 | tf_op jit(solution)/shard_map/all_gather | solution.py:99
  10.4 21.9 %collective-permute-start = (bf16[1,2,16,256]{3,2,1,0:T(8,128)(2,1)S(1)}, bf16[1,2,16,256]{3,2,1,0:T(8,128)(2,1)S(1)}, u32[]{:S(2)}, u32[]{:S(2)}) collective-permute-start(bf16[1,2,16,256]{3,2,1,0:T(8,128)(2,1)S(1)} %get-tuple-element.10), channel_id=1, source_target_pairs={{0,16},{16,32},{32,48},{48,64},{64,80},{80,96},{96,112},{1,17},{17... | collective-permute-start | bytes 49160 | tf_op jit(solution)/shard_map/ppermute | solution.py:23
  15.3 17.9 %collective-permute-start.1 = (bf16[1,2,16,256]{3,2,1,0:T(8,128)(2,1)S(1)}, bf16[1,2,16,256]{3,2,1,0:T(8,128)(2,1)S(1)}, u32[]{:S(2)}, u32[]{:S(2)}) collective-permute-start(bf16[1,2,16,256]{3,2,1,0:T(8,128)(2,1)S(1)} %get-tuple-element.9), channel_id=1, source_target_pairs={{16,0},{32,16},{48,32},{64,48},{80,64},{96,80},{112,96},{17,1},{33... | collective-permute-start | bytes 49160 | tf_op jit(solution)/shard_map/ppermute | solution.py:25
  17.2 10.6 %collective-permute-start.5 = (bf16[2,2,16,64]{3,2,1,0:T(8,128)(2,1)S(1)}, bf16[2,2,16,64]{3,2,1,0:T(8,128)(2,1)S(1)}, u32[]{:S(2)}, u32[]{:S(2)}) collective-permute-start(bf16[2,2,16,64]{3,2,1,0:T(8,128)(2,1)S(1)} %get-tuple-element.12), channel_id=1, source_target_pairs={{16,0},{32,16},{48,32},{64,48},{80,64},{96,80},{112,96},{17,1},{33... | collective-permute-start | bytes 24584 | tf_op jit(solution)/shard_map/ppermute | solution.py:25
  19.2 8.7 %collective-permute-start.4 = (bf16[2,2,16,64]{3,2,1,0:T(8,128)(2,1)S(1)}, bf16[2,2,16,64]{3,2,1,0:T(8,128)(2,1)S(1)}, u32[]{:S(2)}, u32[]{:S(2)}) collective-permute-start(bf16[2,2,16,64]{3,2,1,0:T(8,128)(2,1)S(1)} %get-tuple-element.11), channel_id=1, source_target_pairs={{0,16},{16,32},{32,48},{48,64},{64,80},{80,96},{96,112},{1,17},{17... | collective-permute-start | bytes 24584 | tf_op jit(solution)/shard_map/ppermute | solution.py:23
  27.9 10.6 %collective-permute-start.6 = (bf16[8,2,16,64]{3,2,1,0:T(8,128)(2,1)S(1)}, bf16[8,2,16,64]{3,2,1,0:T(8,128)(2,1)S(1)}, u32[]{:S(2)}, u32[]{:S(2)}) collective-permute-start(bf16[8,2,16,64]{3,2,1,0:T(8,128)(2,1)S(1)} %pad_maximum_fusion.5), channel_id=1, source_target_pairs={{0,1},{1,2},{2,3},{3,4},{4,5},{5,6},{6,7},{7,8},{8,9},{9,10},{10,1... | collective-permute-start | bytes 98312 | tf_op jit(solution)/shard_map/ppermute | solution.py:23
  31.0 7.5 %collective-permute-start.7 = (bf16[8,2,16,64]{3,2,1,0:T(8,128)(2,1)S(1)}, bf16[8,2,16,64]{3,2,1,0:T(8,128)(2,1)S(1)}, u32[]{:S(2)}, u32[]{:S(2)}) collective-permute-start(bf16[8,2,16,64]{3,2,1,0:T(8,128)(2,1)S(1)} %pad_maximum_fusion.5), channel_id=1, source_target_pairs={{1,0},{2,1},{3,2},{4,3},{5,4},{6,5},{7,6},{8,7},{9,8},{10,9},{11,1... | collective-permute-start | bytes 98312 | tf_op jit(solution)/shard_map/ppermute | solution.py:25
  33.2 6.3 %collective-permute-start.2 = (bf16[6,1,16,256]{3,2,1,0:T(8,128)(2,1)S(1)}, bf16[6,1,16,256]{3,2,1,0:T(8,128)(2,1)S(1)}, u32[]{:S(2)}, u32[]{:S(2)}) collective-permute-start(bf16[6,1,16,256]{3,2,1,0:T(8,128)(2,1)S(1)} %get-tuple-element.6), channel_id=1, source_target_pairs={{0,1},{1,2},{2,3},{3,4},{4,5},{5,6},{6,7},{7,8},{8,9},{9,10},{10,1... | collective-permute-start | bytes 147464 | tf_op jit(solution)/shard_map/ppermute | solution.py:23
  37.2 5.6 %collective-permute-start.3 = (bf16[6,1,16,256]{3,2,1,0:T(8,128)(2,1)S(1)}, bf16[6,1,16,256]{3,2,1,0:T(8,128)(2,1)S(1)}, u32[]{:S(2)}, u32[]{:S(2)}) collective-permute-start(bf16[6,1,16,256]{3,2,1,0:T(8,128)(2,1)S(1)} %get-tuple-element.5), channel_id=1, source_target_pairs={{1,0},{2,1},{3,2},{4,3},{5,4},{6,5},{7,6},{8,7},{9,8},{10,9},{11,1... | collective-permute-start | bytes 147464 | tf_op jit(solution)/shard_map/ppermute | solution.py:25
  38.7 0.9 copy-start.1
  42.9 36.4 %copy-start.4 = (s32[1,8]{1,0:T(1,128)S(1)}, s32[1,8]{1,0:T(1,128)}, u32[]{:S(2)}) copy-start(s32[1,8]{1,0:T(1,128)} %param.16) | copy-start | bytes 100
  79.3 4.4 %copy-start.2 = (bf16[4,2,256,64]{2,3,1,0:T(8,128)(2,1)S(1)}, bf16[4,2,256,64]{2,3,1,0:T(8,128)(2,1)}, u32[]{:S(2)}) copy-start(bf16[4,2,256,64]{2,3,1,0:T(8,128)(2,1)} %param.13) | copy-start | bytes 786436
  79.3 4.4 %copy-start.3 = (bf16[4,2,64,256]{3,2,1,0:T(8,128)(2,1)S(1)}, bf16[4,2,64,256]{3,2,1,0:T(8,128)(2,1)}, u32[]{:S(2)}) copy-start(bf16[4,2,64,256]{3,2,1,0:T(8,128)(2,1)} %param.15) | copy-start | bytes 786436
Sparse Core Ops, SparseCore 0:
  10.3 68.9 all-gather.2
where the time goes:
time: 92.2 us; the launch traced here: 91.6 us
  waiting for transfers between devices  35.1 us (38%)
  starting transfers between devices  22.1 us (24%)
  between operations  13.8 us (15%)
  matrix products  13.6 us (15%)
  local copies, waits for them, and re-layouts  5.3 us (6%)
  other arithmetic  1.72 us (2%)
    all_gather x1, waiting for transfers between devices, per_device(): lax.all_gather(coarse_own[None], ('row', 'col'), axis=0, tiled=True)  31.8 us
    ppermute x4, starting transfers between devices, extended(): lax.ppermute(tail, axis, [(i, (i + 1) % count) for i in range(ends)])  15.7 us
    ppermute x4, starting transfers between devices, extended(): lax.ppermute(head, axis, [((i + 1) % count, i) for i in range(ends)])  6.43 us
    dot_general x1, matrix products, per_device(): jnp.einsum('xysrl,xyslm->xyrm', stacked_near, near_blocks, preferred_elem...  4.58 us
    dot_general x1, matrix products, per_device(): jnp.einsum('fd,drj->frj', selector, all_coarse, precision=lax.Precision.H...  3.5 us
    ppermute x4, waiting for transfers between devices, extended(): lax.ppermute(head, axis, [((i + 1) % count, i) for i in range(ends)])  3.25 us
    unnamed x42, local copies, waits for them, and re-layouts  1.86 us
  transfers between devices with their start and end apart: 9, of which 2 were waited for; matrix products, arithmetic and copies ran while one was open for 13% of the time, Pallas kernels for 0%

commit v1 on v0

v1 whole, which is shorter than its diff:
```python
import jax
import jax.numpy as jnp
from jax import lax
from jax.experimental import pallas as pl
from jax.experimental.pallas import tpu as pltpu
from jax.sharding import PartitionSpec as P

MESH = pl.DeviceIdType.MESH
LX, LY, RHS, LEAF, RANK, COARSE, FAR2 = 4, 2, 16, 256, 64, 256, 8
N_ROW, N_COL = 8, 16
NEAR_OFFSETS = [(a, b) for a in (-1, 0, 1) for b in (-1, 0, 1)]
FAR_OFFSETS = [(a, b) for a in range(-2, 3) for b in range(-2, 3) if (a, b) != (0, 0)]
RING1 = [(a, b) for a, b in NEAR_OFFSETS if (a, b) != (0, 0)]
RING2 = FAR_OFFSETS
BF16, F32 = jnp.bfloat16, jnp.float32


def dot(lhs, rhs):
    return lax.dot_general(lhs, rhs, (((1,), (0,)), ((), ())), preferred_element_type=F32)


def dot_t(lhs, rhs):
    return lax.dot_general(lhs, rhs, (((1,), (1,)), ((), ())), preferred_element_type=F32)


def halo_part(a, b, width):
    src, size, dst = [], [], []
    for step, own in ((a, LX), (b, LY)):
        size.append(own if step == 0 else width)
        src.append(own - width if step == 1 else 0)
        dst.append({-1: width + own, 0: width, 1: 0}[step])
    return src, size, dst


def kernel(
    vec_hbm, near_hbm, near_mask_hbm, far_mask_hbm, leaf_hbm, transfer_hbm, cbasis_hbm, clist_hbm, ctrans_hbm,
    out_ref,
    vecs, coef, coarse, nblk, leafb, ftr, cbasis, ctr, ctr_hi, ctr_lo, near_acc, weights,
    near_mask, far_mask, clist,
    near_sem, load_sem, vec_send, vec_recv, coef_send, coef_recv, coarse_send, coarse_recv,
):
    row = lax.axis_index("row")
    col = lax.axis_index("col")

    def at(a, b):
        return (row + a, col + b)

    def when_there(a, b):
        r, c = at(a, b)
        return pl.when((r >= 0) & (r < N_ROW) & (c >= 0) & (c < N_COL))

    load_leaf = pltpu.make_async_copy(leaf_hbm, leafb, load_sem.at[0])
    load_leaf.start()
    load_cbasis = pltpu.make_async_copy(cbasis_hbm, cbasis, load_sem.at[1])
    load_cbasis.start()

    vecs[...] = jnp.zeros_like(vecs)
    coef[...] = jnp.zeros_like(coef)

    barrier = pltpu.get_barrier_semaphore()
    for a, b in RING2:
        @when_there(a, b)
        def _():
            pl.semaphore_signal(barrier, inc=1, device_id=at(a, b), device_id_type=MESH)

    load_vec = pltpu.make_async_copy(vec_hbm, vecs.at[pl.ds(1, LX), pl.ds(1, LY)], load_sem.at[2])
    load_vec.start()
    load_small = []
    for k, (src, dst) in enumerate(((near_mask_hbm, near_mask), (far_mask_hbm, far_mask), (clist_hbm, clist))):
        load_small.append(pltpu.make_async_copy(src, dst, load_sem.at[5 + k]))
        load_small[-1].start()
    load_ctr = pltpu.make_async_copy(ctrans_hbm, ctr, load_sem.at[3])
    load_near = []
    for p in range(LX * LY):
        load_near.append(pltpu.make_async_copy(near_hbm.at[p // LY, p % LY], nblk.at[p], near_sem.at[p]))
        load_near[-1].start()
        if p == 0:
            load_ctr.start()
    load_ftr = pltpu.make_async_copy(transfer_hbm, ftr, load_sem.at[4])
    load_ftr.start()

    row_count = jnp.minimum(row, 2) + jnp.minimum(N_ROW - 1 - row, 2) + 1
    col_count = jnp.minimum(col, 2) + jnp.minimum(N_COL - 1 - col, 2) + 1
    pl.semaphore_wait(barrier, row_count * col_count - 1)

    def vec_copy(a, b):
        src, size, dst = halo_part(a, b, 1)
        k = RING1.index((a, b))
        return pltpu.make_async_remote_copy(
            src_ref=vecs.at[pl.ds(1 + src[0], size[0]), pl.ds(1 + src[1], size[1])],
            dst_ref=vecs.at[pl.ds(dst[0], size[0]), pl.ds(dst[1], size[1])],
            send_sem=vec_send.at[k], recv_sem=vec_recv.at[k], device_id=at(a, b), device_id_type=MESH,
        )

    def coef_copy(a, b):
        src, size, dst = halo_part(a, b, 2)
        k = RING1.index((a, b))
        return pltpu.make_async_remote_copy(
            src_ref=coef.at[pl.ds(2 + src[0], size[0]), pl.ds(2 + src[1], size[1])],
            dst_ref=coef.at[pl.ds(dst[0], size[0]), pl.ds(dst[1], size[1])],
            send_sem=coef_send.at[k], recv_sem=coef_recv.at[k], device_id=at(a, b), device_id_type=MESH,
        )

    def coarse_copy(a, b):
        slot = (2 - a) * 5 + 2 - b
        return pltpu.make_async_remote_copy(
            src_ref=coarse.at[12], dst_ref=coarse.at[slot],
            send_sem=coarse_send.at[slot], recv_sem=coarse_recv.at[slot], device_id=at(a, b), device_id_type=MESH,
        )

    load_vec.wait()
    for a, b in RING1:
        @when_there(a, b)
        def _():
            vec_copy(a, b).start()

    load_leaf.wait()
    for p in range(LX * LY):
        i, j = p // LY, p % LY
        coef[2 + i, 2 + j] = dot_t(vecs[1 + i, 1 + j], leafb[i, j]).astype(BF16)
    for a, b in RING1:
        @when_there(a, b)
        def _():
            coef_copy(a, b).start()

    load_cbasis.wait()
    own = jnp.zeros((RHS, COARSE), F32)
    for p in range(LX * LY):
        i, j = p // LY, p % LY
        own += dot(coef[2 + i, 2 + j], cbasis[i, j])
    coarse[12] = own
    for a, b in RING2:
        @when_there(a, b)
        def _():
            coarse_copy(a, b).start()

    for copy in load_small:
        copy.wait()
    for o, (a, b) in enumerate(FAR_OFFSETS):
        ring = [x for x in FAR_OFFSETS if (max(abs(x[0]), abs(x[1])) == 1) == (max(abs(a), abs(b)) == 1)].index((a, b))
        for p in range(LX * LY):
            i, j = p // LY, p % LY
            if max(abs(a), abs(b)) == 1:
                w = 1 - near_mask[i, j, ring]
            else:
                w = far_mask[i, j, ring]
            weights[o, p] = jnp.full((RHS, RANK), w.astype(F32), F32).astype(BF16)

    def near_term(p, s):
        i, j = p // LY, p % LY
        a, b = NEAR_OFFSETS[s]
        lhs = vecs[1 + i + a, 1 + j + b]
        if s != 4:
            live = near_mask[i, j, s if s < 4 else s - 1]
            lhs = lhs * jnp.full((RHS, LEAF), live.astype(F32), F32).astype(BF16)
        return dot(lhs, nblk[p, s])

    def inside(p, s):
        a, b = NEAR_OFFSETS[s]
        return 0 <= p // LY + a < LX and 0 <= p % LY + b < LY

    for p in range(LX * LY):
        load_near[p].wait()
        near_acc[p] = sum(near_term(p, s) for s in range(9) if inside(p, s))

    load_ctr.wait()
    for f in range(FAR2):
        whole = ctr[f]
        hi = whole.astype(BF16)
        ctr_hi[f] = hi
        ctr_lo[f] = (whole - hi.astype(F32)).astype(BF16)

    for a, b in RING1:
        @when_there(a, b)
        def _():
            vec_copy(-a, -b).wait_recv()
    for p in range(LX * LY):
        outer = [s for s in range(9) if not inside(p, s)]
        if outer:
            near_acc[p] += sum(near_term(p, s) for s in outer)

    load_ftr.wait()
    for a, b in RING1:
        @when_there(a, b)
        def _():
            coef_copy(-a, -b).wait_recv()
    local = jnp.zeros((LX * LY * RHS, RANK), F32)
    for o, (a, b) in enumerate(FAR_OFFSETS):
        lhs = coef[2 + a : 2 + a + LX, 2 + b : 2 + b + LY].reshape(LX * LY, RHS, RANK) * weights[o]
        local += dot(lhs.reshape(LX * LY * RHS, RANK), ftr[o])

    for a, b in RING1:
        @when_there(a, b)
        def _():
            vec_copy(a, b).wait_send()
            coef_copy(a, b).wait_send()
    for a, b in RING2:
        @when_there(a, b)
        def _():
            coarse_copy(a, b).wait_send()
    for a, b in RING2:
        @when_there(a, b)
        def _():
            coarse_copy(-a, -b).wait_recv()

    total = jnp.zeros((RHS, COARSE), F32)
    for f in range(FAR2):
        listed = clist[0, f]
        slot = (listed // N_COL - row + 2) * 5 + listed % N_COL - col + 2
        whole = coarse[jnp.clip(slot, 0, 24)]
        hi = whole.astype(BF16)
        lo = (whole - hi.astype(F32)).astype(BF16)
        total += dot(hi, ctr_hi[f]) + (dot(lo, ctr_hi[f]) + dot(hi, ctr_lo[f]))
    coarse_local = total.astype(BF16)
    for p in range(LX * LY):
        i, j = p // LY, p % LY
        down = dot_t(coarse_local, cbasis[i, j])
        both = (local[p * RHS : (p + 1) * RHS] + down).astype(BF16)
        out_ref[i, j] = near_acc[p] + dot(both, leafb[i, j])


def per_device(vectors, near_blocks, near_mask, far_mask, leaf_basis, far_transfer, coarse_basis, coarse_list, coarse_transfer):
    any_ = pl.BlockSpec(memory_space=pltpu.HBM)
    vmem = pl.BlockSpec(memory_space=pltpu.VMEM)
    dma = pltpu.SemaphoreType.DMA
    operands = [
        pltpu.with_memory_space_constraint(x, pltpu.HBM)
        for x in (
            vectors, near_blocks, near_mask, far_mask, leaf_basis.swapaxes(2, 3), far_transfer, coarse_basis, coarse_list,
            coarse_transfer[0],
        )
    ]
    return pl.pallas_call(
        kernel,
        out_shape=jax.ShapeDtypeStruct((LX, LY, RHS, LEAF), F32),
        in_specs=[any_] * 9,
        out_specs=vmem,
        scratch_shapes=[
            pltpu.VMEM((LX + 2, LY + 2, RHS, LEAF), BF16),
            pltpu.VMEM((LX + 4, LY + 4, RHS, RANK), BF16),
            pltpu.VMEM((25, RHS, COARSE), F32),
            pltpu.VMEM((LX * LY, 9, LEAF, LEAF), BF16),
            pltpu.VMEM((LX, LY, RANK, LEAF), BF16),
            pltpu.VMEM((24, RANK, RANK), BF16),
            pltpu.VMEM((LX, LY, RANK, COARSE), BF16),
            pltpu.VMEM((FAR2, COARSE, COARSE), F32),
            pltpu.VMEM((FAR2, COARSE, COARSE), BF16),
            pltpu.VMEM((FAR2, COARSE, COARSE), BF16),
            pltpu.VMEM((LX * LY, RHS, LEAF), F32),
            pltpu.VMEM((24, LX * LY, RHS, RANK), BF16),
            pltpu.SMEM((LX, LY, 8), jnp.int32),
            pltpu.SMEM((LX, LY, 16), jnp.int32),
            pltpu.SMEM((1, FAR2), jnp.int32),
            dma((LX * LY,)),
            dma((8,)),
            dma((8,)),
            dma((8,)),
            dma((8,)),
            dma((8,)),
            dma((25,)),
            dma((25,)),
        ],
        compiler_params=pltpu.CompilerParams(
            collective_id=0, has_side_effects=True, vmem_limit_bytes=40 * 1024 * 1024
        ),
    )(*operands)


def solution(mesh):
    placed = (
        P("row", "col", None, None),
        P("row", "col", None, None, None),
        P("row", "col", None),
        P("row", "col", None),
        P("row", "col", None, None),
        P(),
        P("row", "col", None, None),
        P(("row", "col"), None),
        P(("row", "col"), None, None, None),
    )
    return jax.shard_map(
        per_device, mesh=mesh, in_specs=placed, out_specs=P("row", "col", None, None), check_vma=False
    )
```

time: 92.2 us -> 19.4 us (0.21)
  the two profiles are of different devices: /device:TPU:1 before, /device:TPU:9 now
where the time goes in v1:
time: 19.4 us; the launch traced here: 19.3 us
  Pallas kernels  18.6 us (96%)
  local copies, waits for them, and re-layouts  0.66 us (3%)
    pallas_call x1, Pallas kernels, per_device(): pl.pallas_call(kernel, out_shape=jax.ShapeDtypeStruct((LX, LY, RHS, LEAF)...  18.6 us
    unnamed x1, local copies, waits for them, and re-layouts  0.66 us

profile of v1, /device:TPU:9, one launch (start us, length us, event | category | flops | bytes accessed | tf_op | source)
XLA Modules:
  0.0 19.3 jit_solution(11781657376598365449)
XLA Ops:
  0.0 18.6 %shard_map.91 = f32[4,2,16,256]{3,2,1,0:T(8,128)S(1)} custom-call(bf16[4,2,16,256]{3,2,1,0:T(8,128)(2,1)} %vec_hbm.1, bf16[4,2,9,256,256]{4,3,2,1,0:T(8,128)(2,1)} %near_hbm.1, s32[4,2,8]{2,1,0:T(2,128)} %near_mask_hbm.1, s32[4,2,16]{2,1,0:T(2,128)} %far_mask_hbm.1, bf16[4,2,64,256]{3,2,1,0:T(8,128)(2,1)} %bitcast.3, bf16[24,64,64]{2,1,0:T(8,128)(2,1)} %transfer_hbm.1, ...), custom_call_target="tpu_custom_call" | custom-call | tf_op jit(solution)/shard_map/pallas_call | solution.py:233
  18.6 0.7 %copy.11 = f32[4,2,16,256]{3,2,1,0:T(8,128)} copy(f32[4,2,16,256]{3,2,1,0:T(8,128)S(1)} %shard_map.91) | data formatting | bytes 262144

commit v2 on v1

--- a/solution.py
+++ b/solution.py
@@ -1,3 +1,5 @@
+import functools
+
 import jax
 import jax.numpy as jnp
 from jax import lax
@@ -11,7 +13,12 @@
 NEAR_OFFSETS = [(a, b) for a in (-1, 0, 1) for b in (-1, 0, 1)]
 FAR_OFFSETS = [(a, b) for a in range(-2, 3) for b in range(-2, 3) if (a, b) != (0, 0)]
 RING1 = [(a, b) for a, b in NEAR_OFFSETS if (a, b) != (0, 0)]
-RING2 = FAR_OFFSETS
+COLS = [(0, -2), (0, 2), (0, -1), (0, 1)]
+ROWS = [(-2, 0), (2, 0), (-1, 0), (1, 0)]
+CORNERS = [(-1, -1), (-1, 1), (1, -1), (1, 1)]
+PARTNERS = COLS + ROWS + CORNERS
+NEAR_FIRST = 6
+PLACE = {0: 0, -2: 1, -1: 2, 1: 3, 2: 4}
 BF16, F32 = jnp.bfloat16, jnp.float32
 
 
@@ -45,26 +52,34 @@
     def at(a, b):
         return (row + a, col + b)
 
-    def when_there(a, b):
+    there = {}
+    for a, b in PARTNERS:
         r, c = at(a, b)
-        return pl.when((r >= 0) & (r < N_ROW) & (c >= 0) & (c < N_COL))
-
+        there[a, b] = (r >= 0) & (r < N_ROW) & (c >= 0) & (c < N_COL)
+
+    def each(offsets, step):
+        for a, b in offsets:
+            pl.when(there[a, b])(functools.partial(step, a, b))
+
+    load_vec = pltpu.make_async_copy(vec_hbm, vecs.at[pl.ds(1, LX), pl.ds(1, LY)], load_sem.at[2])
+    load_vec.start()
     load_leaf = pltpu.make_async_copy(leaf_hbm, leafb, load_sem.at[0])
     load_leaf.start()
     load_cbasis = pltpu.make_async_copy(cbasis_hbm, cbasis, load_sem.at[1])
     load_cbasis.start()
 
-    vecs[...] = jnp.zeros_like(vecs)
-    coef[...] = jnp.zeros_like(coef)
+    for ref, width, last in ((vecs, 1, LEAF), (coef, 2, RANK)):
+        edge = jnp.zeros((width, LY + 2 * width, RHS, last), BF16)
+        side = jnp.zeros((LX, width, RHS, last), BF16)
+        ref[0:width] = edge
+        ref[width + LX : 2 * width + LX] = edge
+        ref[width : width + LX, 0:width] = side
+        ref[width : width + LX, width + LY : 2 * width + LY] = side
+    coarse[2, 1:5] = jnp.zeros((4, RHS, COARSE), F32)
 
     barrier = pltpu.get_barrier_semaphore()
-    for a, b in RING2:
-        @when_there(a, b)
-        def _():
-            pl.semaphore_signal(barrier, inc=1, device_id=at(a, b), device_id_type=MESH)
-
-    load_vec = pltpu.make_async_copy(vec_hbm, vecs.at[pl.ds(1, LX), pl.ds(1, LY)], load_sem.at[2])
-    load_vec.start()
+    each(PARTNERS, lambda a, b: pl.semaphore_signal(barrier, inc=1, device_id=at(a, b), device_id_type=MESH))
+
     load_small = []
     for k, (src, dst) in enumerate(((near_mask_hbm, near_mask), (far_mask_hbm, far_mask), (clist_hbm, clist))):
         load_small.append(pltpu.make_async_copy(src, dst, load_sem.at[5 + k]))
@@ -79,10 +94,6 @@
     load_ftr = pltpu.make_async_copy(transfer_hbm, ftr, load_sem.at[4])
     load_ftr.start()
 
-    row_count = jnp.minimum(row, 2) + jnp.minimum(N_ROW - 1 - row, 2) + 1
-    col_count = jnp.minimum(col, 2) + jnp.minimum(N_COL - 1 - col, 2) + 1
-    pl.semaphore_wait(barrier, row_count * col_count - 1)
-
     def vec_copy(a, b):
         src, size, dst = halo_part(a, b, 1)
         k = RING1.index((a, b))
@@ -101,38 +112,47 @@
             send_sem=coef_send.at[k], recv_sem=coef_recv.at[k], device_id=at(a, b), device_id_type=MESH,
         )
 
-    def coarse_copy(a, b):
-        slot = (2 - a) * 5 + 2 - b
-        return pltpu.make_async_remote_copy(
-            src_ref=coarse.at[12], dst_ref=coarse.at[slot],
-            send_sem=coarse_send.at[slot], recv_sem=coarse_recv.at[slot], device_id=at(a, b), device_id_type=MESH,
+    def col_copy(a, b):
+        place = PLACE[-b]
+        return pltpu.make_async_remote_copy(
+            src_ref=coarse.at[2, 0], dst_ref=coarse.at[2, place],
+            send_sem=coarse_send.at[0, place], recv_sem=coarse_recv.at[0, place], device_id=at(a, b), device_id_type=MESH,
+        )
+
+    def row_copy(a, b):
+        place = PLACE[-a]
+        return pltpu.make_async_remote_copy(
+            src_ref=coarse.at[2, 0], dst_ref=coarse.at[2 - a, 0],
+            send_sem=coarse_send.at[1, place], recv_sem=coarse_recv.at[1, place], device_id=at(a, b), device_id_type=MESH,
+        )
+
+    def hand_on(a, b):
+        place = PLACE[-a]
+        return pltpu.make_async_remote_copy(
+            src_ref=coarse.at[2, pl.ds(1, 4)], dst_ref=coarse.at[2 - a, pl.ds(1, 4)],
+            send_sem=coarse_send.at[2, place], recv_sem=coarse_recv.at[2, place], device_id=at(a, b), device_id_type=MESH,
         )
 
     load_vec.wait()
-    for a, b in RING1:
-        @when_there(a, b)
-        def _():
-            vec_copy(a, b).start()
-
     load_leaf.wait()
     for p in range(LX * LY):
         i, j = p // LY, p % LY
         coef[2 + i, 2 + j] = dot_t(vecs[1 + i, 1 + j], leafb[i, j]).astype(BF16)
-    for a, b in RING1:
-        @when_there(a, b)
-        def _():
-            coef_copy(a, b).start()
-
     load_cbasis.wait()
     own = jnp.zeros((RHS, COARSE), F32)
     for p in range(LX * LY):
         i, j = p // LY, p % LY
         own += dot(coef[2 + i, 2 + j], cbasis[i, j])
-    coarse[12] = own
-    for a, b in RING2:
-        @when_there(a, b)
-        def _():
-            coarse_copy(a, b).start()
+    coarse[2, 0] = own
+
+    above, below = jnp.minimum(row, 2), jnp.minimum(N_ROW - 1 - row, 2)
+    ahead, behind = jnp.minimum(col, 2), jnp.minimum(N_COL - 1 - col, 2)
+    corners = (jnp.minimum(row, 1) + jnp.minimum(N_ROW - 1 - row, 1)) * (jnp.minimum(col, 1) + jnp.minimum(N_COL - 1 - col, 1))
+    pl.semaphore_wait(barrier, above + below + ahead + behind + corners)
+    each(COLS, lambda a, b: col_copy(a, b).start())
+    each(ROWS, lambda a, b: row_copy(a, b).start())
+    each(RING1, lambda a, b: vec_copy(a, b).start())
+    each(RING1, lambda a, b: coef_copy(a, b).start())
 
     for copy in load_small:
         copy.wait()
@@ -160,6 +180,9 @@
         return 0 <= p // LY + a < LX and 0 <= p % LY + b < LY
 
     for p in range(LX * LY):
+        if p == NEAR_FIRST:
+            each(COLS, lambda a, b: col_copy(-a, -b).wait_recv())
+            each(ROWS, lambda a, b: hand_on(a, b).start())
         load_near[p].wait()
         near_acc[p] = sum(near_term(p, s) for s in range(9) if inside(p, s))
 
@@ -170,44 +193,28 @@
         ctr_hi[f] = hi
         ctr_lo[f] = (whole - hi.astype(F32)).astype(BF16)
 
-    for a, b in RING1:
-        @when_there(a, b)
-        def _():
-            vec_copy(-a, -b).wait_recv()
+    each(RING1, lambda a, b: vec_copy(-a, -b).wait_recv())
     for p in range(LX * LY):
         outer = [s for s in range(9) if not inside(p, s)]
         if outer:
             near_acc[p] += sum(near_term(p, s) for s in outer)
 
     load_ftr.wait()
-    for a, b in RING1:
-        @when_there(a, b)
-        def _():
-            coef_copy(-a, -b).wait_recv()
+    each(RING1, lambda a, b: coef_copy(-a, -b).wait_recv())
     local = jnp.zeros((LX * LY * RHS, RANK), F32)
     for o, (a, b) in enumerate(FAR_OFFSETS):
         lhs = coef[2 + a : 2 + a + LX, 2 + b : 2 + b + LY].reshape(LX * LY, RHS, RANK) * weights[o]
         local += dot(lhs.reshape(LX * LY * RHS, RANK), ftr[o])
 
-    for a, b in RING1:
-        @when_there(a, b)
-        def _():
-            vec_copy(a, b).wait_send()
-            coef_copy(a, b).wait_send()
-    for a, b in RING2:
-        @when_there(a, b)
-        def _():
-            coarse_copy(a, b).wait_send()
-    for a, b in RING2:
-        @when_there(a, b)
-        def _():
-            coarse_copy(-a, -b).wait_recv()
+    each(ROWS, lambda a, b: row_copy(-a, -b).wait_recv())
+    each(ROWS, lambda a, b: hand_on(-a, -b).wait_recv())
 
     total = jnp.zeros((RHS, COARSE), F32)
     for f in range(FAR2):
         listed = clist[0, f]
-        slot = (listed // N_COL - row + 2) * 5 + listed % N_COL - col + 2
-        whole = coarse[jnp.clip(slot, 0, 24)]
+        step_b = listed % N_COL - col
+        place = jnp.where(step_b == 0, 0, jnp.where(step_b < 0, step_b + 3, step_b + 2))
+        whole = coarse[jnp.clip(listed // N_COL - row + 2, 0, 4), jnp.clip(place, 0, 4)]
         hi = whole.astype(BF16)
         lo = (whole - hi.astype(F32)).astype(BF16)
         total += dot(hi, ctr_hi[f]) + (dot(lo, ctr_hi[f]) + dot(hi, ctr_lo[f]))
@@ -217,6 +224,12 @@
         down = dot_t(coarse_local, cbasis[i, j])
         both = (local[p * RHS : (p + 1) * RHS] + down).astype(BF16)
         out_ref[i, j] = near_acc[p] + dot(both, leafb[i, j])
+
+    each(RING1, lambda a, b: vec_copy(a, b).wait_send())
+    each(RING1, lambda a, b: coef_copy(a, b).wait_send())
+    each(COLS, lambda a, b: col_copy(a, b).wait_send())
+    each(ROWS, lambda a, b: row_copy(a, b).wait_send())
+    each(ROWS, lambda a, b: hand_on(a, b).wait_send())
 
 
 def per_device(vectors, near_blocks, near_mask, far_mask, leaf_basis, far_transfer, coarse_basis, coarse_list, coarse_transfer):
@@ -238,7 +251,7 @@
         scratch_shapes=[
             pltpu.VMEM((LX + 2, LY + 2, RHS, LEAF), BF16),
             pltpu.VMEM((LX + 4, LY + 4, RHS, RANK), BF16),
-            pltpu.VMEM((25, RHS, COARSE), F32),
+            pltpu.VMEM((5, 5, RHS, COARSE), F32),
             pltpu.VMEM((LX * LY, 9, LEAF, LEAF), BF16),
             pltpu.VMEM((LX, LY, RANK, LEAF), BF16),
             pltpu.VMEM((24, RANK, RANK), BF16),
@@ -257,8 +270,8 @@
             dma((8,)),
             dma((8,)),
             dma((8,)),
-            dma((25,)),
-            dma((25,)),
+            dma((3, 5)),
+            dma((3, 5)),
         ],
         compiler_params=pltpu.CompilerParams(
             collective_id=0, has_side_effects=True, vmem_limit_bytes=40 * 1024 * 1024

time: 19.4 us -> 15.9 us (0.82)
  the two profiles are of different devices: /device:TPU:9 before, /device:TPU:1 now
where the time goes in v2:
time: 15.9 us; the launch traced here: 15.8 us
  Pallas kernels  15.1 us (95%)
  local copies, waits for them, and re-layouts  0.66 us (4%)
    pallas_call x1, Pallas kernels, per_device(): pl.pallas_call(kernel, out_shape=jax.ShapeDtypeStruct((LX, LY, RHS, LEAF)...  15.1 us
    unnamed x1, local copies, waits for them, and re-layouts  0.66 us

profile of v2, /device:TPU:1, one launch (start us, length us, event | category | flops | bytes accessed | tf_op | source)
XLA Modules:
  0.0 15.8 jit_solution(6050114624726924153)
XLA Ops:
  0.0 15.1 %shard_map.91 = f32[4,2,16,256]{3,2,1,0:T(8,128)S(1)} custom-call(bf16[4,2,16,256]{3,2,1,0:T(8,128)(2,1)} %vec_hbm.1, bf16[4,2,9,256,256]{4,3,2,1,0:T(8,128)(2,1)} %near_hbm.1, s32[4,2,8]{2,1,0:T(2,128)} %near_mask_hbm.1, s32[4,2,16]{2,1,0:T(2,128)} %far_mask_hbm.1, bf16[4,2,64,256]{3,2,1,0:T(8,128)(2,1)} %bitcast.3, bf16[24,64,64]{2,1,0:T(8,128)(2,1)} %transfer_hbm.1, ...), custom_call_target="tpu_custom_call" | custom-call | tf_op jit(solution)/shard_map/pallas_call | solution.py:246
  15.1 0.7 %copy.11 = f32[4,2,16,256]{3,2,1,0:T(8,128)} copy(f32[4,2,16,256]{3,2,1,0:T(8,128)S(1)} %shard_map.91) | data formatting | bytes 262144

commit v3 on v2

--- a/solution.py
+++ b/solution.py
@@ -61,24 +61,15 @@
         for a, b in offsets:
             pl.when(there[a, b])(functools.partial(step, a, b))
 
+    barrier = pltpu.get_barrier_semaphore()
+    each(PARTNERS, lambda a, b: pl.semaphore_signal(barrier, inc=1, device_id=at(a, b), device_id_type=MESH))
+
     load_vec = pltpu.make_async_copy(vec_hbm, vecs.at[pl.ds(1, LX), pl.ds(1, LY)], load_sem.at[2])
     load_vec.start()
     load_leaf = pltpu.make_async_copy(leaf_hbm, leafb, load_sem.at[0])
     load_leaf.start()
     load_cbasis = pltpu.make_async_copy(cbasis_hbm, cbasis, load_sem.at[1])
     load_cbasis.start()
-
-    for ref, width, last in ((vecs, 1, LEAF), (coef, 2, RANK)):
-        edge = jnp.zeros((width, LY + 2 * width, RHS, last), BF16)
-        side = jnp.zeros((LX, width, RHS, last), BF16)
-        ref[0:width] = edge
-        ref[width + LX : 2 * width + LX] = edge
-        ref[width : width + LX, 0:width] = side
-        ref[width : width + LX, width + LY : 2 * width + LY] = side
-    coarse[2, 1:5] = jnp.zeros((4, RHS, COARSE), F32)
-
-    barrier = pltpu.get_barrier_semaphore()
-    each(PARTNERS, lambda a, b: pl.semaphore_signal(barrier, inc=1, device_id=at(a, b), device_id_type=MESH))
 
     load_small = []
     for k, (src, dst) in enumerate(((near_mask_hbm, near_mask), (far_mask_hbm, far_mask), (clist_hbm, clist))):
@@ -94,6 +85,23 @@
     load_ftr = pltpu.make_async_copy(transfer_hbm, ftr, load_sem.at[4])
     load_ftr.start()
 
+    for ref, width, last in ((vecs, 1, LEAF), (coef, 2, RANK)):
+        edge = (width, LY + 2 * width, RHS, last)
+        side = (LX + 2 * width, width, RHS, last)
+        for missing, place, shape in (
+            (row == 0, (pl.ds(0, width),), edge),
+            (row == N_ROW - 1, (pl.ds(width + LX, width),), edge),
+            (col == 0, (slice(None), pl.ds(0, width)), side),
+            (col == N_COL - 1, (slice(None), pl.ds(width + LY, width)), side),
+        ):
+            @pl.when(missing)
+            def _():
+                ref[place] = jnp.zeros(shape, BF16)
+    for a, b in COLS:
+        @pl.when(jnp.logical_not(there[a, b]))
+        def _():
+            coarse[2, PLACE[b]] = jnp.zeros((RHS, COARSE), F32)
+
     def vec_copy(a, b):
         src, size, dst = halo_part(a, b, 1)
         k = RING1.index((a, b))
@@ -135,14 +143,12 @@
 
     load_vec.wait()
     load_leaf.wait()
-    for p in range(LX * LY):
-        i, j = p // LY, p % LY
-        coef[2 + i, 2 + j] = dot_t(vecs[1 + i, 1 + j], leafb[i, j]).astype(BF16)
+    leaf = [(p // LY, p % LY) for p in range(LX * LY)]
+    coeffs = [dot_t(vecs[1 + i, 1 + j], leafb[i, j]).astype(BF16) for i, j in leaf]
+    for (i, j), value in zip(leaf, coeffs):
+        coef[2 + i, 2 + j] = value
     load_cbasis.wait()
-    own = jnp.zeros((RHS, COARSE), F32)
-    for p in range(LX * LY):
-        i, j = p // LY, p % LY
-        own += dot(coef[2 + i, 2 + j], cbasis[i, j])
+    own = sum(dot(value, cbasis[i, j]) for (i, j), value in zip(leaf, coeffs))
     coarse[2, 0] = own
 
     above, below = jnp.minimum(row, 2), jnp.minimum(N_ROW - 1 - row, 2)
@@ -210,6 +216,7 @@
     each(ROWS, lambda a, b: hand_on(-a, -b).wait_recv())
 
     total = jnp.zeros((RHS, COARSE), F32)
+    both = jnp.zeros((2 * RHS, COARSE), F32)
     for f in range(FAR2):
         listed = clist[0, f]
         step_b = listed % N_COL - col
@@ -217,13 +224,16 @@
         whole = coarse[jnp.clip(listed // N_COL - row + 2, 0, 4), jnp.clip(place, 0, 4)]
         hi = whole.astype(BF16)
         lo = (whole - hi.astype(F32)).astype(BF16)
-        total += dot(hi, ctr_hi[f]) + (dot(lo, ctr_hi[f]) + dot(hi, ctr_lo[f]))
+        both += dot(jnp.concatenate([hi, lo], axis=0), ctr_hi[f])
+        total += dot(hi, ctr_lo[f])
+    total = both[:RHS] + (both[RHS:] + total)
     coarse_local = total.astype(BF16)
+    down = [dot_t(coarse_local, cbasis[p // LY, p % LY]) for p in range(LX * LY)]
+    whole = [(local[p * RHS : (p + 1) * RHS] + down[p]).astype(BF16) for p in range(LX * LY)]
+    far = [dot(whole[p], leafb[p // LY, p % LY]) for p in range(LX * LY)]
+    applied = [near_acc[p] + far[p] for p in range(LX * LY)]
     for p in range(LX * LY):
-        i, j = p // LY, p % LY
-        down = dot_t(coarse_local, cbasis[i, j])
-        both = (local[p * RHS : (p + 1) * RHS] + down).astype(BF16)
-        out_ref[i, j] = near_acc[p] + dot(both, leafb[i, j])
+        out_ref[p // LY, p % LY] = applied[p]
 
     each(RING1, lambda a, b: vec_copy(a, b).wait_send())
     each(RING1, lambda a, b: coef_copy(a, b).wait_send())

time: 15.9 us -> 15.2 us (0.956)
  Pallas kernels: 15.1 us -> 14.4 us
    pallas_call x1, Pallas kernels: 15.1 us -> 14.4 us  [per_device(): pl.pallas_call(kernel, out_shape=jax.ShapeDtypeStruct((LX, LY, RHS, LEAF)...]
where the time goes in v3:
time: 15.2 us; the launch traced here: 15.1 us
  Pallas kernels  14.4 us (95%)
  local copies, waits for them, and re-layouts  0.66 us (4%)
    pallas_call x1, Pallas kernels, per_device(): pl.pallas_call(kernel, out_shape=jax.ShapeDtypeStruct((LX, LY, RHS, LEAF)...  14.4 us
    unnamed x1, local copies, waits for them, and re-layouts  0.66 us

profile of v3, /device:TPU:1, one launch (start us, length us, event | category | flops | bytes accessed | tf_op | source)
XLA Modules:
  0.0 15.1 jit_solution(9052796465818059193)
XLA Ops:
  0.0 14.4 %shard_map.91 = f32[4,2,16,256]{3,2,1,0:T(8,128)S(1)} custom-call(bf16[4,2,16,256]{3,2,1,0:T(8,128)(2,1)} %vec_hbm.1, bf16[4,2,9,256,256]{4,3,2,1,0:T(8,128)(2,1)} %near_hbm.1, s32[4,2,8]{2,1,0:T(2,128)} %near_mask_hbm.1, s32[4,2,16]{2,1,0:T(2,128)} %far_mask_hbm.1, bf16[4,2,64,256]{3,2,1,0:T(8,128)(2,1)} %bitcast.3, bf16[24,64,64]{2,1,0:T(8,128)(2,1)} %transfer_hbm.1, ...), custom_call_target="tpu_custom_call" | custom-call | tf_op jit(solution)/shard_map/pallas_call | solution.py:256
  14.4 0.7 %copy.11 = f32[4,2,16,256]{3,2,1,0:T(8,128)} copy(f32[4,2,16,256]{3,2,1,0:T(8,128)S(1)} %shard_map.91) | data formatting | bytes 262144

commit v4 on v3

--- a/solution.py
+++ b/solution.py
@@ -19,7 +19,9 @@
 PARTNERS = COLS + ROWS + CORNERS
 NEAR_FIRST = 6
 PLACE = {0: 0, -2: 1, -1: 2, 1: 3, 2: 4}
-BF16, F32 = jnp.bfloat16, jnp.float32
+BF16, F32, I16, I32 = jnp.bfloat16, jnp.float32, jnp.int16, jnp.int32
+MESSAGE = COARSE + 128
+LEAST = 2.0**-100
 
 
 def dot(lhs, rhs):
@@ -37,6 +39,20 @@
         src.append(own - width if step == 1 else 0)
         dst.append({-1: width + own, 0: width, 1: 0}[step])
     return src, size, dst
+
+
+def encoded(values):
+    largest = jnp.max(jnp.abs(values), axis=1, keepdims=True)
+    exponent = jnp.floor(jnp.log2(jnp.maximum(largest, LEAST))) + 1.0
+    whole = jnp.clip(jnp.round(values * jnp.exp2(15.0 - exponent)), -32767.0, 32767.0)
+    tail = jnp.broadcast_to(exponent, (RHS, MESSAGE - COARSE))
+    return jnp.concatenate([whole, tail], axis=1).astype(I32).astype(I16)
+
+
+def decoded(message):
+    numbers = message.astype(I32).astype(F32)
+    scale = jnp.exp2(numbers[:, COARSE:] - 15.0)
+    return numbers[:, :COARSE] * jnp.concatenate([scale] * (COARSE // scale.shape[1]), axis=1)
 
 
 def kernel(
@@ -100,7 +116,7 @@
     for a, b in COLS:
         @pl.when(jnp.logical_not(there[a, b]))
         def _():
-            coarse[2, PLACE[b]] = jnp.zeros((RHS, COARSE), F32)
+            coarse[2, PLACE[b]] = jnp.zeros((RHS, MESSAGE), I16)
 
     def vec_copy(a, b):
         src, size, dst = halo_part(a, b, 1)
@@ -134,12 +150,20 @@
             send_sem=coarse_send.at[1, place], recv_sem=coarse_recv.at[1, place], device_id=at(a, b), device_id_type=MESH,
         )
 
-    def hand_on(a, b):
+    def hand_on(side, a, b):
         place = PLACE[-a]
-        return pltpu.make_async_remote_copy(
-            src_ref=coarse.at[2, pl.ds(1, 4)], dst_ref=coarse.at[2 - a, pl.ds(1, 4)],
-            send_sem=coarse_send.at[2, place], recv_sem=coarse_recv.at[2, place], device_id=at(a, b), device_id_type=MESH,
-        )
+        pair = pl.ds(1 + 2 * side, 2)
+        return pltpu.make_async_remote_copy(
+            src_ref=coarse.at[2, pair], dst_ref=coarse.at[2 - a, pair],
+            send_sem=coarse_send.at[2 + side, place], recv_sem=coarse_recv.at[2 + side, place],
+            device_id=at(a, b), device_id_type=MESH,
+        )
+
+    has_side = (col > 0, col < N_COL - 1)
+
+    def each_side(side, step):
+        for a, b in ROWS:
+            pl.when(there[a, b] & has_side[side])(functools.partial(step, side, a, b))
 
     load_vec.wait()
     load_leaf.wait()
@@ -149,7 +173,7 @@
         coef[2 + i, 2 + j] = value
     load_cbasis.wait()
     own = sum(dot(value, cbasis[i, j]) for (i, j), value in zip(leaf, coeffs))
-    coarse[2, 0] = own
+    coarse[2, 0] = encoded(own)
 
     above, below = jnp.minimum(row, 2), jnp.minimum(N_ROW - 1 - row, 2)
     ahead, behind = jnp.minimum(col, 2), jnp.minimum(N_COL - 1 - col, 2)
@@ -187,8 +211,9 @@
 
     for p in range(LX * LY):
         if p == NEAR_FIRST:
-            each(COLS, lambda a, b: col_copy(-a, -b).wait_recv())
-            each(ROWS, lambda a, b: hand_on(a, b).start())
+            for side in (0, 1):
+                each([k for k in COLS if (k[1] > 0) == side], lambda a, b: col_copy(-a, -b).wait_recv())
+                each_side(side, lambda side, a, b: hand_on(side, a, b).start())
         load_near[p].wait()
         near_acc[p] = sum(near_term(p, s) for s in range(9) if inside(p, s))
 
@@ -212,8 +237,13 @@
         lhs = coef[2 + a : 2 + a + LX, 2 + b : 2 + b + LY].reshape(LX * LY, RHS, RANK) * weights[o]
         local += dot(lhs.reshape(LX * LY * RHS, RANK), ftr[o])
 
+    each(RING1, lambda a, b: vec_copy(a, b).wait_send())
+    each(RING1, lambda a, b: coef_copy(a, b).wait_send())
+    each(COLS, lambda a, b: col_copy(a, b).wait_send())
+    each(ROWS, lambda a, b: row_copy(a, b).wait_send())
     each(ROWS, lambda a, b: row_copy(-a, -b).wait_recv())
-    each(ROWS, lambda a, b: hand_on(-a, -b).wait_recv())
+    for side in (0, 1):
+        each_side(side, lambda side, a, b: hand_on(side, -a, -b).wait_recv())
 
     total = jnp.zeros((RHS, COARSE), F32)
     both = jnp.zeros((2 * RHS, COARSE), F32)
@@ -221,7 +251,7 @@
         listed = clist[0, f]
         step_b = listed % N_COL - col
         place = jnp.where(step_b == 0, 0, jnp.where(step_b < 0, step_b + 3, step_b + 2))
-        whole = coarse[jnp.clip(listed // N_COL - row + 2, 0, 4), jnp.clip(place, 0, 4)]
+        whole = decoded(coarse[jnp.clip(listed // N_COL - row + 2, 0, 4), jnp.clip(place, 0, 4)])
         hi = whole.astype(BF16)
         lo = (whole - hi.astype(F32)).astype(BF16)
         both += dot(jnp.concatenate([hi, lo], axis=0), ctr_hi[f])
@@ -235,11 +265,8 @@
     for p in range(LX * LY):
         out_ref[p // LY, p % LY] = applied[p]
 
-    each(RING1, lambda a, b: vec_copy(a, b).wait_send())
-    each(RING1, lambda a, b: coef_copy(a, b).wait_send())
-    each(COLS, lambda a, b: col_copy(a, b).wait_send())
-    each(ROWS, lambda a, b: row_copy(a, b).wait_send())
-    each(ROWS, lambda a, b: hand_on(a, b).wait_send())
+    for side in (0, 1):
+        each_side(side, lambda side, a, b: hand_on(side, a, b).wait_send())
 
 
 def per_device(vectors, near_blocks, near_mask, far_mask, leaf_basis, far_transfer, coarse_basis, coarse_list, coarse_transfer):
@@ -261,7 +288,7 @@
         scratch_shapes=[
             pltpu.VMEM((LX + 2, LY + 2, RHS, LEAF), BF16),
             pltpu.VMEM((LX + 4, LY + 4, RHS, RANK), BF16),
-            pltpu.VMEM((5, 5, RHS, COARSE), F32),
+            pltpu.VMEM((5, 5, RHS, MESSAGE), I16),
             pltpu.VMEM((LX * LY, 9, LEAF, LEAF), BF16),
             pltpu.VMEM((LX, LY, RANK, LEAF), BF16),
             pltpu.VMEM((24, RANK, RANK), BF16),
@@ -280,8 +307,8 @@
             dma((8,)),
             dma((8,)),
             dma((8,)),
-            dma((3, 5)),
-            dma((3, 5)),
+            dma((4, 5)),
+            dma((4, 5)),
         ],
         compiler_params=pltpu.CompilerParams(
             collective_id=0, has_side_effects=True, vmem_limit_bytes=40 * 1024 * 1024

time: 15.2 us -> 14.5 us (0.954); the launches traced: 15.1 us -> 14.2 us
  Pallas kernels: 14.4 us -> 13.6 us
    pallas_call x1, Pallas kernels: 14.4 us -> 13.6 us  [per_device(): pl.pallas_call(kernel, out_shape=jax.ShapeDtypeStruct((LX, LY, RHS, LEAF)...]
where the time goes in v4:
time: 14.5 us; the launch traced here: 14.2 us
  Pallas kernels  13.6 us (94%)
  local copies, waits for them, and re-layouts  0.66 us (5%)
    pallas_call x1, Pallas kernels, per_device(): pl.pallas_call(kernel, out_shape=jax.ShapeDtypeStruct((LX, LY, RHS, LEAF)...  13.6 us
    unnamed x1, local copies, waits for them, and re-layouts  0.66 us

profile of v4, /device:TPU:1, one launch (start us, length us, event | category | flops | bytes accessed | tf_op | source)
XLA Modules:
  0.0 14.2 jit_solution(12696878026511388425)
XLA Ops:
  0.0 13.6 %shard_map.91 = f32[4,2,16,256]{3,2,1,0:T(8,128)S(1)} custom-call(bf16[4,2,16,256]{3,2,1,0:T(8,128)(2,1)} %vec_hbm.1, bf16[4,2,9,256,256]{4,3,2,1,0:T(8,128)(2,1)} %near_hbm.1, s32[4,2,8]{2,1,0:T(2,128)} %near_mask_hbm.1, s32[4,2,16]{2,1,0:T(2,128)} %far_mask_hbm.1, bf16[4,2,64,256]{3,2,1,0:T(8,128)(2,1)} %bitcast.3, bf16[24,64,64]{2,1,0:T(8,128)(2,1)} %transfer_hbm.1, ...), custom_call_target="tpu_custom_call" | custom-call | tf_op jit(solution)/shard_map/pallas_call | solution.py:283
  13.6 0.7 %copy.11 = f32[4,2,16,256]{3,2,1,0:T(8,128)} copy(f32[4,2,16,256]{3,2,1,0:T(8,128)S(1)} %shard_map.91) | data formatting | bytes 262144

commit v5 on v4

--- a/solution.py
+++ b/solution.py
@@ -16,8 +16,9 @@
 COLS = [(0, -2), (0, 2), (0, -1), (0, 1)]
 ROWS = [(-2, 0), (2, 0), (-1, 0), (1, 0)]
 CORNERS = [(-1, -1), (-1, 1), (1, -1), (1, 1)]
-PARTNERS = COLS + ROWS + CORNERS
-NEAR_FIRST = 6
+PARTNERS = COLS + ROWS
+SIDES = [(-1, 0), (1, 0), (0, -1), (0, 1)]
+NEAR_FIRST = 3
 PLACE = {0: 0, -2: 1, -1: 2, 1: 3, 2: 4}
 BF16, F32, I16, I32 = jnp.bfloat16, jnp.float32, jnp.int16, jnp.int32
 MESSAGE = COARSE + 128
@@ -60,7 +61,7 @@
     out_ref,
     vecs, coef, coarse, nblk, leafb, ftr, cbasis, ctr, ctr_hi, ctr_lo, near_acc, weights,
     near_mask, far_mask, clist,
-    near_sem, load_sem, vec_send, vec_recv, coef_send, coef_recv, coarse_send, coarse_recv,
+    near_sem, load_sem, vec_send, vec_recv, coef_send, coef_recv, coarse_send, coarse_recv, ready,
 ):
     row = lax.axis_index("row")
     col = lax.axis_index("col")
@@ -69,7 +70,7 @@
         return (row + a, col + b)
 
     there = {}
-    for a, b in PARTNERS:
+    for a, b in PARTNERS + CORNERS:
         r, c = at(a, b)
         there[a, b] = (r >= 0) & (r < N_ROW) & (c >= 0) & (c < N_COL)
 
@@ -91,16 +92,6 @@
     for k, (src, dst) in enumerate(((near_mask_hbm, near_mask), (far_mask_hbm, far_mask), (clist_hbm, clist))):
         load_small.append(pltpu.make_async_copy(src, dst, load_sem.at[5 + k]))
         load_small[-1].start()
-    load_ctr = pltpu.make_async_copy(ctrans_hbm, ctr, load_sem.at[3])
-    load_near = []
-    for p in range(LX * LY):
-        load_near.append(pltpu.make_async_copy(near_hbm.at[p // LY, p % LY], nblk.at[p], near_sem.at[p]))
-        load_near[-1].start()
-        if p == 0:
-            load_ctr.start()
-    load_ftr = pltpu.make_async_copy(transfer_hbm, ftr, load_sem.at[4])
-    load_ftr.start()
-
     for ref, width, last in ((vecs, 1, LEAF), (coef, 2, RANK)):
         edge = (width, LY + 2 * width, RHS, last)
         side = (LX + 2 * width, width, RHS, last)
@@ -172,17 +163,30 @@
     for (i, j), value in zip(leaf, coeffs):
         coef[2 + i, 2 + j] = value
     load_cbasis.wait()
+    load_ctr = pltpu.make_async_copy(ctrans_hbm, ctr, load_sem.at[3])
+    load_near = []
+    for p in range(LX * LY):
+        load_near.append(pltpu.make_async_copy(near_hbm.at[p // LY, p % LY], nblk.at[p], near_sem.at[p]))
+        load_near[-1].start()
+        if p == 0:
+            load_ctr.start()
+    load_ftr = pltpu.make_async_copy(transfer_hbm, ftr, load_sem.at[4])
+    load_ftr.start()
     own = sum(dot(value, cbasis[i, j]) for (i, j), value in zip(leaf, coeffs))
     coarse[2, 0] = encoded(own)
 
     above, below = jnp.minimum(row, 2), jnp.minimum(N_ROW - 1 - row, 2)
     ahead, behind = jnp.minimum(col, 2), jnp.minimum(N_COL - 1 - col, 2)
-    corners = (jnp.minimum(row, 1) + jnp.minimum(N_ROW - 1 - row, 1)) * (jnp.minimum(col, 1) + jnp.minimum(N_COL - 1 - col, 1))
-    pl.semaphore_wait(barrier, above + below + ahead + behind + corners)
+    pl.semaphore_wait(barrier, above + below + ahead + behind)
+
+    each(SIDES[:2], lambda a, b: pl.semaphore_signal(ready, inc=1, device_id=at(a, b), device_id_type=MESH))
     each(COLS, lambda a, b: col_copy(a, b).start())
     each(ROWS, lambda a, b: row_copy(a, b).start())
-    each(RING1, lambda a, b: vec_copy(a, b).start())
-    each(RING1, lambda a, b: coef_copy(a, b).start())
+    each(SIDES, lambda a, b: vec_copy(a, b).start())
+    each(SIDES, lambda a, b: coef_copy(a, b).start())
+    pl.semaphore_wait(ready, jnp.minimum(row, 1) + jnp.minimum(N_ROW - 1 - row, 1))
+    each(CORNERS, lambda a, b: vec_copy(a, b).start())
+    each(CORNERS, lambda a, b: coef_copy(a, b).start())
 
     for copy in load_small:
         copy.wait()
@@ -309,6 +313,7 @@
             dma((8,)),
             dma((4, 5)),
             dma((4, 5)),
+            pltpu.SemaphoreType.REGULAR,
         ],
         compiler_params=pltpu.CompilerParams(
             collective_id=0, has_side_effects=True, vmem_limit_bytes=40 * 1024 * 1024

time: 14.5 us -> 14.2 us (0.979)
  Pallas kernels: 13.6 us -> 13.3 us
    pallas_call x1, Pallas kernels: 13.6 us -> 13.3 us  [per_device(): pl.pallas_call(kernel, out_shape=jax.ShapeDtypeStruct((LX, LY, RHS, LEAF)...]
where the time goes in v5:
time: 14.2 us; the launch traced here: 14 us
  Pallas kernels  13.3 us (94%)
  local copies, waits for them, and re-layouts  0.66 us (5%)
    pallas_call x1, Pallas kernels, per_device(): pl.pallas_call(kernel, out_shape=jax.ShapeDtypeStruct((LX, LY, RHS, LEAF)...  13.3 us
    unnamed x1, local copies, waits for them, and re-layouts  0.66 us

profile of v5, /device:TPU:1, one launch (start us, length us, event | category | flops | bytes accessed | tf_op | source)
XLA Modules:
  0.0 14.0 jit_solution(10124281762078517477)
XLA Ops:
  0.0 13.3 %shard_map.91 = f32[4,2,16,256]{3,2,1,0:T(8,128)S(1)} custom-call(bf16[4,2,16,256]{3,2,1,0:T(8,128)(2,1)} %vec_hbm.1, bf16[4,2,9,256,256]{4,3,2,1,0:T(8,128)(2,1)} %near_hbm.1, s32[4,2,8]{2,1,0:T(2,128)} %near_mask_hbm.1, s32[4,2,16]{2,1,0:T(2,128)} %far_mask_hbm.1, bf16[4,2,64,256]{3,2,1,0:T(8,128)(2,1)} %bitcast.3, bf16[24,64,64]{2,1,0:T(8,128)(2,1)} %transfer_hbm.1, ...), custom_call_target="tpu_custom_call" | custom-call | tf_op jit(solution)/shard_map/pallas_call | solution.py:287
  13.3 0.7 %copy.11 = f32[4,2,16,256]{3,2,1,0:T(8,128)} copy(f32[4,2,16,256]{3,2,1,0:T(8,128)S(1)} %shard_map.91) | data formatting | bytes 262144

commit v6 on v5

--- a/solution.py
+++ b/solution.py
@@ -13,10 +13,10 @@
 NEAR_OFFSETS = [(a, b) for a in (-1, 0, 1) for b in (-1, 0, 1)]
 FAR_OFFSETS = [(a, b) for a in range(-2, 3) for b in range(-2, 3) if (a, b) != (0, 0)]
 RING1 = [(a, b) for a, b in NEAR_OFFSETS if (a, b) != (0, 0)]
-COLS = [(0, -2), (0, 2), (0, -1), (0, 1)]
-ROWS = [(-2, 0), (2, 0), (-1, 0), (1, 0)]
+COLS = [(0, -2), (0, 2), (0, 1), (0, -1)]
+ROWS = [(-1, 0), (-2, 0), (2, 0), (1, 0)]
 CORNERS = [(-1, -1), (-1, 1), (1, -1), (1, 1)]
-PARTNERS = COLS + ROWS
+PARTNERS = [(-1, 0), (-2, 0), (0, -2), (0, -1), (0, 2), (0, 1), (1, 0), (2, 0)]
 SIDES = [(-1, 0), (1, 0), (0, -1), (0, 1)]
 NEAR_FIRST = 3
 PLACE = {0: 0, -2: 1, -1: 2, 1: 3, 2: 4}
@@ -215,7 +215,7 @@
 
     for p in range(LX * LY):
         if p == NEAR_FIRST:
-            for side in (0, 1):
+            for side in (1, 0):
                 each([k for k in COLS if (k[1] > 0) == side], lambda a, b: col_copy(-a, -b).wait_recv())
                 each_side(side, lambda side, a, b: hand_on(side, a, b).start())
         load_near[p].wait()
@@ -246,7 +246,7 @@
     each(COLS, lambda a, b: col_copy(a, b).wait_send())
     each(ROWS, lambda a, b: row_copy(a, b).wait_send())
     each(ROWS, lambda a, b: row_copy(-a, -b).wait_recv())
-    for side in (0, 1):
+    for side in (1, 0):
         each_side(side, lambda side, a, b: hand_on(side, -a, -b).wait_recv())
 
     total = jnp.zeros((RHS, COARSE), F32)

time: 14.2 us -> 13.8 us (0.972); the launches traced: 14 us -> 13.7 us
  Pallas kernels: 13.3 us -> 13.1 us
    pallas_call x1, Pallas kernels: 13.3 us -> 13.1 us  [per_device(): pl.pallas_call(kernel, out_shape=jax.ShapeDtypeStruct((LX, LY, RHS, LEAF)...]
where the time goes in v6:
time: 13.8 us; the launch traced here: 13.7 us
  Pallas kernels  13.1 us (95%)
  local copies, waits for them, and re-layouts  0.66 us (5%)
    pallas_call x1, Pallas kernels, per_device(): pl.pallas_call(kernel, out_shape=jax.ShapeDtypeStruct((LX, LY, RHS, LEAF)...  13.1 us
    unnamed x1, local copies, waits for them, and re-layouts  0.66 us

profile of v6, /device:TPU:1, one launch (start us, length us, event | category | flops | bytes accessed | tf_op | source)
XLA Modules:
  0.0 13.7 jit_solution(3306914208465149581)
XLA Ops:
  0.0 13.1 %shard_map.91 = f32[4,2,16,256]{3,2,1,0:T(8,128)S(1)} custom-call(bf16[4,2,16,256]{3,2,1,0:T(8,128)(2,1)} %vec_hbm.1, bf16[4,2,9,256,256]{4,3,2,1,0:T(8,128)(2,1)} %near_hbm.1, s32[4,2,8]{2,1,0:T(2,128)} %near_mask_hbm.1, s32[4,2,16]{2,1,0:T(2,128)} %far_mask_hbm.1, bf16[4,2,64,256]{3,2,1,0:T(8,128)(2,1)} %bitcast.3, bf16[24,64,64]{2,1,0:T(8,128)(2,1)} %transfer_hbm.1, ...), custom_call_target="tpu_custom_call" | custom-call | tf_op jit(solution)/shard_map/pallas_call | solution.py:287
  13.1 0.7 %copy.11 = f32[4,2,16,256]{3,2,1,0:T(8,128)} copy(f32[4,2,16,256]{3,2,1,0:T(8,128)S(1)} %shard_map.91) | data formatting | bytes 262144

commit v7 on v6

--- a/solution.py
+++ b/solution.py
@@ -78,15 +78,15 @@
         for a, b in offsets:
             pl.when(there[a, b])(functools.partial(step, a, b))
 
-    barrier = pltpu.get_barrier_semaphore()
-    each(PARTNERS, lambda a, b: pl.semaphore_signal(barrier, inc=1, device_id=at(a, b), device_id_type=MESH))
-
     load_vec = pltpu.make_async_copy(vec_hbm, vecs.at[pl.ds(1, LX), pl.ds(1, LY)], load_sem.at[2])
     load_vec.start()
     load_leaf = pltpu.make_async_copy(leaf_hbm, leafb, load_sem.at[0])
     load_leaf.start()
     load_cbasis = pltpu.make_async_copy(cbasis_hbm, cbasis, load_sem.at[1])
     load_cbasis.start()
+
+    barrier = pltpu.get_barrier_semaphore()
+    each(PARTNERS, lambda a, b: pl.semaphore_signal(barrier, inc=1, device_id=at(a, b), device_id_type=MESH))
 
     load_small = []
     for k, (src, dst) in enumerate(((near_mask_hbm, near_mask), (far_mask_hbm, far_mask), (clist_hbm, clist))):

time: 13.8 us -> 13.8 us (level)
  no operation moved by 1% of the time
where the time goes in v7:
time: 13.8 us; the launch traced here: 13.7 us
  Pallas kernels  13.1 us (95%)
  local copies, waits for them, and re-layouts  0.66 us (5%)
    pallas_call x1, Pallas kernels, per_device(): pl.pallas_call(kernel, out_shape=jax.ShapeDtypeStruct((LX, LY, RHS, LEAF)...  13.1 us
    unnamed x1, local copies, waits for them, and re-layouts  0.66 us

profile of v7, /device:TPU:1, one launch (start us, length us, event | category | flops | bytes accessed | tf_op | source)
XLA Modules:
  0.0 13.7 jit_solution(14278557768359620203)
XLA Ops:
  0.0 13.1 %shard_map.91 = f32[4,2,16,256]{3,2,1,0:T(8,128)S(1)} custom-call(bf16[4,2,16,256]{3,2,1,0:T(8,128)(2,1)} %vec_hbm.1, bf16[4,2,9,256,256]{4,3,2,1,0:T(8,128)(2,1)} %near_hbm.1, s32[4,2,8]{2,1,0:T(2,128)} %near_mask_hbm.1, s32[4,2,16]{2,1,0:T(2,128)} %far_mask_hbm.1, bf16[4,2,64,256]{3,2,1,0:T(8,128)(2,1)} %bitcast.3, bf16[24,64,64]{2,1,0:T(8,128)(2,1)} %transfer_hbm.1, ...), custom_call_target="tpu_custom_call" | custom-call | tf_op jit(solution)/shard_map/pallas_call | solution.py:287
  13.1 0.7 %copy.11 = f32[4,2,16,256]{3,2,1,0:T(8,128)} copy(f32[4,2,16,256]{3,2,1,0:T(8,128)S(1)} %shard_map.91) | data formatting | bytes 262144

commit v8 on v6

--- a/solution.py
+++ b/solution.py
@@ -14,7 +14,7 @@
 FAR_OFFSETS = [(a, b) for a in range(-2, 3) for b in range(-2, 3) if (a, b) != (0, 0)]
 RING1 = [(a, b) for a, b in NEAR_OFFSETS if (a, b) != (0, 0)]
 COLS = [(0, -2), (0, 2), (0, 1), (0, -1)]
-ROWS = [(-1, 0), (-2, 0), (2, 0), (1, 0)]
+ROWS = [(-1, 0), (-2, 0), (1, 0), (2, 0)]
 CORNERS = [(-1, -1), (-1, 1), (1, -1), (1, 1)]
 PARTNERS = [(-1, 0), (-2, 0), (0, -2), (0, -1), (0, 2), (0, 1), (1, 0), (2, 0)]
 SIDES = [(-1, 0), (1, 0), (0, -1), (0, 1)]

time: 13.8 us -> 13.8 us (level)
  no operation moved by 1% of the time
where the time goes in v8:
time: 13.8 us; the launch traced here: 13.7 us
  Pallas kernels  13.1 us (95%)
  local copies, waits for them, and re-layouts  0.66 us (5%)
    pallas_call x1, Pallas kernels, per_device(): pl.pallas_call(kernel, out_shape=jax.ShapeDtypeStruct((LX, LY, RHS, LEAF)...  13.1 us
    unnamed x1, local copies, waits for them, and re-layouts  0.66 us

profile of v8, /device:TPU:1, one launch (start us, length us, event | category | flops | bytes accessed | tf_op | source)
XLA Modules:
  0.0 13.7 jit_solution(3659595005618917960)
XLA Ops:
  0.0 13.1 %shard_map.91 = f32[4,2,16,256]{3,2,1,0:T(8,128)S(1)} custom-call(bf16[4,2,16,256]{3,2,1,0:T(8,128)(2,1)} %vec_hbm.1, bf16[4,2,9,256,256]{4,3,2,1,0:T(8,128)(2,1)} %near_hbm.1, s32[4,2,8]{2,1,0:T(2,128)} %near_mask_hbm.1, s32[4,2,16]{2,1,0:T(2,128)} %far_mask_hbm.1, bf16[4,2,64,256]{3,2,1,0:T(8,128)(2,1)} %bitcast.3, bf16[24,64,64]{2,1,0:T(8,128)(2,1)} %transfer_hbm.1, ...), custom_call_target="tpu_custom_call" | custom-call | tf_op jit(solution)/shard_map/pallas_call | solution.py:287
  13.1 0.7 %copy.11 = f32[4,2,16,256]{3,2,1,0:T(8,128)} copy(f32[4,2,16,256]{3,2,1,0:T(8,128)S(1)} %shard_map.91) | data formatting | bytes 262144
